TPU v7x, 32 devices: a whole 2x2x4 slice. The times are simulated.
32 devices in a mesh: group: 4 (over y, core), fsdp: 8 (over z, x).
Axes of the slice: x: 2, y: 2, z: 4, core: 2. Of those that a mesh axis runs over, the one named last changes fastest.
Arguments:
- anchor: bfloat16 [8192, 1024], P('fsdp'), may hold values from -6 to 6
- pseudo_grads: bfloat16 [4, 8192, 1024], P('group', 'fsdp'), may hold values from -1.5 to 1.5
- outer_moment: float32 [8192, 1024], P('fsdp'), may hold values from -1.2 to 1.2
- adam_first: float32 [4, 8192, 1024], P('group', 'fsdp'), may hold values from -1.8 to 1.8
- adam_second: float32 [4, 8192, 1024], P('group', 'fsdp'), may hold values from 0.25 to 4
- inputs: bfloat16 [8192, 8192], P(('group', 'fsdp')), may hold values from -6 to 6
- key_cotangent: bfloat16 [8192, 1024], P(('group', 'fsdp')), may hold values from -6 to 6
Outputs:
- new_anchor: bfloat16 [8192, 1024], P('fsdp')
- new_moment: float32 [8192, 1024], P('fsdp')
- inner_weights: bfloat16 [4, 8192, 1024], P('group', 'fsdp')
- first_moment: float32 [4, 8192, 1024], P('group', 'fsdp')
- second_moment: float32 [4, 8192, 1024], P('group', 'fsdp')
- input_grad: bfloat16 [8192, 8192], P(('group', 'fsdp'))
All inputs are finite; a program needn't handle non-finite values.
Results may differ from a plain program's by a relative error of at most 0.012.
Values may be sent and summed in bfloat16 or wider, within the bound.
A program may use at most 128 MiB of HBM per device.

v0:
```python
import jax
import jax.numpy as jnp
from jax import lax
from jax.sharding import PartitionSpec as P

OUTER_RATE = 0.7
MOMENTUM = 0.9
INNER_RATE = 0.05
BETA_ONE = 0.9
BETA_TWO = 0.95
ADAM_EPS = 1e-08
DECAY = 0.1
ADAM_STEP = 100


def per_device(anchor, pseudo_grads, outer_moment, adam_first, adam_second, inputs, key_cotangent):
    width = inputs.shape[1]
    scale = width ** (-0.5)
    workers = lax.axis_size("group")
    total = lax.psum(pseudo_grads[0].astype(jnp.float32).astype(jnp.bfloat16), "group").astype(
        jnp.float32
    )
    mean_delta = total / workers
    new_moment = MOMENTUM * outer_moment + mean_delta
    new_anchor = (
        anchor.astype(jnp.float32) - OUTER_RATE * (mean_delta + MOMENTUM * new_moment)
    ).astype(jnp.bfloat16)
    product = jnp.einsum(
        "tk,dk->td",
        key_cotangent,
        lax.all_gather(new_anchor, "fsdp", axis=0, tiled=True),
        preferred_element_type=jnp.float32,
    )
    input_grad = (product * scale).astype(jnp.bfloat16)
    grads = lax.psum_scatter(
        (
            jnp.einsum("td,tk->dk", inputs, key_cotangent, preferred_element_type=jnp.float32)
            * scale
        ).astype(jnp.bfloat16),
        "fsdp",
        scatter_dimension=0,
        tiled=True,
    ).astype(jnp.float32)
    correct_one = 1.0 - BETA_ONE**ADAM_STEP
    correct_two = 1.0 - BETA_TWO**ADAM_STEP
    first_moment = BETA_ONE * adam_first[0] + (1.0 - BETA_ONE) * grads
    second_moment = BETA_TWO * adam_second[0] + (1.0 - BETA_TWO) * grads * grads
    step_size = first_moment / correct_one / (jnp.sqrt(second_moment / correct_two) + ADAM_EPS)
    inner_weights = (
        new_anchor.astype(jnp.float32) * (1.0 - INNER_RATE * DECAY) - INNER_RATE * step_size
    ).astype(jnp.bfloat16)
    return (
        new_anchor,
        new_moment,
        inner_weights[None],
        first_moment[None],
        second_moment[None],
        input_grad,
    )


def solution(mesh):
    return jax.shard_map(
        per_device,
        mesh=mesh,
        in_specs=(
            P("fsdp", None),
            P("group", "fsdp", None),
            P("fsdp", None),
            P("group", "fsdp", None),
            P("group", "fsdp", None),
            P(("group", "fsdp"), None),
            P(("group", "fsdp"), None),
        ),
        out_specs=(
            P("fsdp", None),
            P("fsdp", None),
            P("group", "fsdp", None),
            P("group", "fsdp", None),
            P("group", "fsdp", None),
            P(("group", "fsdp"), None),
        ),
        check_vma=False,
    )
```

profile of v0, /device:TPU:0, one launch (start us, length us, event | category | flops | bytes accessed | tf_op | source)
XLA Modules:
  0.0 565.7 jit_solution(5001839511518046305)
XLA Ops:
  8.0 0.0 copy-start
  8.0 0.0 all-reduce.2.cloned.1.call-start
  8.1 0.7 all-reduce.2.cloned.1.call-update
  8.7 0.0 reduce-scatter.2.cloned.1.call-start
  8.8 0.2 copy-done
  9.0 10.7 %multiply_convert_fusion = bf16[8192,1024]{1,0:T(8,128)(2,1)} fusion(bf16[256,8192]{1,0:T(8,128)(2,1)} %param.12, bf16[256,1024]{1,0:T(8,128)(2,1)S(1)} %copy-done), kind=kOutput, calls=%fused_computation | convolution fusion | flops 4311744512 | bytes 21495808 | tf_op jit(solution)/shard_map/td,tk->dk/dot_general | solution.py:37
  19.7 0.0 copy-start.1
  19.7 0.0 reduce-scatter.2.cloned.1.call-update
  19.7 0.0 all-gather.2.cloned.1.call-start
  19.8 45.7 %all-reduce.2.cloned.1.call-done = bf16[1024,1024]{1,0:T(8,128)(2,1)} async-done(((bf16[1024,1024]{1,0:T(8,128)(2,1)}), bf16[1024,1024]{1,0:T(8,128)(2,1)}) %all-reduce.2.cloned.1.call-update) | async-done | bytes 2097168 | tf_op jit(solution)/shard_map/psum | solution.py:20
  65.5 236.5 %reduce-scatter.2.cloned.1.call-done = bf16[1024,1024]{1,0:T(8,128)(2,1)} async-done(((bf16[8192,1024]{1,0:T(8,128)(2,1)}), bf16[1024,1024]{1,0:T(8,128)(2,1)}) %reduce-scatter.2.cloned.1.call-update) | async-done | bytes 2097168 | tf_op jit(solution)/shard_map/reduce_scatter | solution.py:35
  302.0 0.0 copy-done.1
  302.0 11.2 %fusion.6 = (bf16[1,1024,1024]{2,1,0:T(8,128)(2,1)}, bf16[1024,1024]{1,0:T(8,128)(2,1)}, f32[1024,1024]{1,0:T(8,128)}, f32[1,1024,1024]{2,1,0:T(8,128)}, f32[1,1024,1024]{2,1,0:T(8,128)}) fusion(f32[1,1024,1024]{2,1,0:T(8,128)} %param.11, bf16[1024,1024]{1,0:T(8,128)(2,1)} %reduce-scatter.2.cloned.1.call-done, f32[1,1024,1024]{2,1,0:T(8,128)} %param.10, ...), kind=kLoop, calls=%fused_computation.14 | loop fusion | flops 28311552 | bytes 35651584 | tf_op jit(solution)/shard_map/broadcast_in_dim | solution.py:55
  313.2 0.0 all-gather.2.cloned.1.call-update
  313.2 226.5 %all-gather.2.cloned.1.call-done = bf16[8192,1024]{1,0:T(8,128)(2,1)} async-done(((bf16[1024,1024]{1,0:T(8,128)(2,1)}), bf16[8192,1024]{1,0:T(8,128)(2,1)}) %all-gather.2.cloned.1.call-update) | async-done | bytes 16777232 | tf_op jit(solution)/shard_map/all_gather | solution.py:31
  539.7 12.3 %fusion.1 = bf16[256,8192]{0,1:T(8,128)(2,1)} fusion(bf16[8192,1024]{1,0:T(8,128)(2,1)} %all-gather.2.cloned.1.call-done, bf16[256,1024]{1,0:T(8,128)(2,1)S(1)} %copy-done), kind=kOutput, calls=%fused_computation.3 | convolution fusion | flops 4299161600 | bytes 21495808 | tf_op jit(solution)/shard_map/tk,dk->td/dot_general | solution.py:28
  552.0 6.3 %copy.13 = bf16[256,8192]{1,0:T(8,128)(2,1)} copy(bf16[256,8192]{0,1:T(8,128)(2,1)} %fusion.1) | data formatting | bytes 8388608
Async XLA Ops:
  8.0 1.0 copy-start
  8.0 57.5 %all-reduce.2.cloned.1.call-start = ((), (), s32[]{:S(2)}) async-start(), calls=%async_computation.1 | async-start | bytes 4194304 | tf_op jit(solution)/shard_map/psum | solution.py:20
  8.7 293.3 %reduce-scatter.2.cloned.1.call-start = ((), (), s32[]{:S(2)}) async-start(), calls=%async_computation.2 | async-start | bytes 18874368 | tf_op jit(solution)/shard_map/reduce_scatter | solution.py:35
  19.7 282.3 %copy-start.1 = (bf16[1024,1024]{1,0:T(8,128)(2,1)S(1)}, bf16[1024,1024]{1,0:T(8,128)(2,1)}, u32[]{:S(2)}) copy-start(bf16[1024,1024]{1,0:T(8,128)(2,1)} %param.7) | copy-start | bytes 6291460
  19.7 520.0 %all-gather.2.cloned.1.call-start = ((), (), s32[]{:S(2)}) async-start(), calls=%async_computation.3 | async-start | bytes 18874368 | tf_op jit(solution)/shard_map/all_gather | solution.py:31
Sparse Core Ops, SparseCore 0:
  11.3 54.0 all-reduce.1
Sparse Core Ops, SparseCore 1:
  19.8 282.1 reduce-scatter.1
  313.3 226.4 all-gather.1
where the time goes:
time: 566 us
  waiting for transfers between devices  509 us (90%)
  matrix products  22.9 us (4%)
  between operations  15.5 us (3%)
  other arithmetic  11.2 us (2%)
  local copies, waits for them, and re-layouts  6.57 us (1%)
    reduce_scatter x1, waiting for transfers between devices, per_device(): lax.psum_scatter((jnp.einsum('td,tk->dk', inputs, key_cotangent, preferre...  237 us
    all_gather x1, waiting for transfers between devices, per_device(): lax.all_gather(new_anchor, 'fsdp', axis=0, tiled=True)  227 us
    psum x1, waiting for transfers between devices, per_device(): lax.psum(pseudo_grads[0].astype(jnp.float32).astype(jnp.bfloat16), 'group')  45.7 us
    dot_general x1, matrix products, per_device(): jnp.einsum('tk,dk->td', key_cotangent, lax.all_gather(new_anchor, 'fsdp',...  12.3 us
  transfers between devices with their start and end apart: 3, of which 3 were waited for; matrix products, arithmetic and copies ran while one was open for 2% of the time, Pallas kernels for 0%

commit v1 on v0

--- a/solution.py
+++ b/solution.py
@@ -1,6 +1,10 @@
+import functools
+
 import jax
 import jax.numpy as jnp
 from jax import lax
+from jax.experimental import pallas as pl
+from jax.experimental.pallas import tpu as pltpu
 from jax.sharding import PartitionSpec as P
 
 OUTER_RATE = 0.7
@@ -12,35 +16,324 @@
 DECAY = 0.1
 ADAM_STEP = 100
 
+TILE = 256
+MESH = pl.DeviceIdType.MESH
+
+
+def ring_to_index(place, n):
+    back = lax.div(place, n // 2)
+    return (1 - back) * 2 * place + back * (2 * n - 1 - 2 * place)
+
+
+def index_to_ring(index, n):
+    column = lax.rem(index, 2)
+    row = lax.div(index, 2)
+    return (1 - column) * row + column * (n - 1 - row)
+
+
+def exchange_kernel(
+    n, scale,
+    pg, anchor, moment, inputs, cot,
+    grads, mean_out, input_grad,
+    rows_in, cots, anchors, pg_in, pg_own, anchor_own, moment_own, means,
+    local_sem,
+    pg_send, pg_recv, x_send, x_recv, cot_send, cot_recv, ring_send, ring_recv,
+    y_send, y_recv, core_send, core_recv, pass_send, pass_recv, mean_send, mean_recv,
+):
+    half = n // 2
+    tokens = inputs.shape[0]
+    shard = anchor.shape[0]
+    part = shard // 4
+    me = lax.axis_index("fsdp")
+    mine = lax.axis_index("group")
+    place = index_to_ring(me, n)
+    right = ring_to_index(lax.rem(place + 1, n), n)
+    left = ring_to_index(lax.rem(place + n - 1, n), n)
+    y, core = lax.div(mine, 2), lax.rem(mine, 2)
+    core_peer = 2 * y + 1 - core
+    y_peer = 2 * (1 - y) + core
+    far_peer = 2 * (1 - y) + 1 - core
+    peers = (core_peer, y_peer, far_peer)
+
+    def owner(slot):
+        return ring_to_index(lax.rem(place + n - slot, n), n)
+
+    def quarter(which):
+        return pl.ds(pl.multiple_of(which * part, part), part)
+
+    def local(src, dst, sem):
+        return pltpu.make_async_copy(src, dst, local_sem.at[sem])
+
+    def remote(src, dst, send, recv, fsdp, group):
+        return pltpu.make_async_remote_copy(
+            src_ref=src, dst_ref=dst, send_sem=send, recv_sem=recv,
+            device_id={"group": group, "fsdp": fsdp}, device_id_type=MESH,
+        )
+
+    def shard_columns(index):
+        return pl.ds(pl.multiple_of(index * shard, shard), shard)
+
+    own_copies = [
+        local(cot, cots.at[0], 0),
+        local(pg.at[0, quarter(mine), :], pg_own, 1),
+        local(anchor.at[quarter(mine), :], anchor_own, 2),
+        local(moment.at[quarter(mine), :], moment_own, 3),
+        local(inputs.at[:, shard_columns(me)], rows_in.at[0], 4),
+    ]
+    for copy in own_copies:
+        copy.start()
+
+    barrier = pltpu.get_barrier_semaphore()
+    for step in range(1, n):
+        pl.semaphore_signal(
+            barrier, inc=1, device_id={"group": mine, "fsdp": owner(step)}, device_id_type=MESH
+        )
+    for peer in peers:
+        pl.semaphore_signal(
+            barrier, inc=1, device_id={"group": peer, "fsdp": me}, device_id_type=MESH
+        )
+    pl.semaphore_wait(barrier, n + 2)
+
+    sent = []
+
+    def send(copy):
+        copy.start()
+        sent.append(copy)
+
+    pg_copies = [
+        remote(pg.at[0, quarter(peer), :], pg_in.at[i], pg_send.at[i], pg_recv.at[i], me, peer)
+        for i, peer in enumerate(peers)
+    ]
+    for i in (1, 2, 0):
+        send(pg_copies[i])
+
+    def ring_step(buffer, rows, first, step, send_sem, recv_sem):
+        if step < half:
+            spans = ((first, rows, step), (first, rows, n - step))
+        else:
+            spans = ((first, rows // 2, half), (first + rows // 2, rows // 2, n))
+        (up, up_rows, up_sem), (down, down_rows, down_sem) = spans
+        up_at = pl.ds(pl.multiple_of(up, rows // 2), up_rows)
+        down_at = pl.ds(pl.multiple_of(down, rows // 2), down_rows)
+        return (
+            remote(
+                buffer.at[step - 1, up_at, :], buffer.at[step, up_at, :],
+                send_sem.at[up_sem], recv_sem.at[up_sem], right, mine,
+            ),
+            remote(
+                buffer.at[(n - step + 1) % n, down_at, :], buffer.at[n - step, down_at, :],
+                send_sem.at[down_sem], recv_sem.at[down_sem], left, mine,
+            ),
+        )
+
+    cot_steps = [None] + [
+        ring_step(cots, tokens, 0, step, cot_send, cot_recv) for step in range(1, half + 1)
+    ]
+    ring_steps = [None] + [
+        ring_step(anchors, part, mine * part, step, ring_send, ring_recv)
+        for step in range(1, half + 1)
+    ]
+
+    own_copies[0].wait()
+    for copy in cot_steps[1]:
+        send(copy)
+
+    x_copies = [None] * n
+    for step in range(1, half + 1):
+        for slot in (step, n - step) if step < half else (half,):
+            target = ring_to_index(lax.rem(place + slot, n), n)
+            x_copies[slot] = remote(
+                inputs.at[:, shard_columns(target)], rows_in.at[slot],
+                x_send.at[slot], x_recv.at[slot], target, mine,
+            )
+            send(x_copies[slot])
+
+    def cot_turn(step):
+        for copy in cot_steps[step]:
+            copy.wait_recv()
+        if step < half:
+            for copy in cot_steps[step + 1]:
+                send(copy)
+
+    def slots_of(step):
+        if step == 0:
+            return (0,)
+        return (step, n - step) if step < half else (half,)
+
+    def over(slot, which, send_sem, recv_sem, peer):
+        view = anchors.at[slot, quarter(which), :]
+        return remote(view, view, send_sem.at[slot], recv_sem.at[slot], me, peer)
+
+    def spread(step):
+        for slot in slots_of(step):
+            send(over(slot, mine, y_send, y_recv, y_peer))
+            send(over(slot, mine, core_send, core_recv, core_peer))
+
+    def hand_on(step):
+        for slot in slots_of(step):
+            over(slot, mine, y_send, y_recv, y_peer).wait_recv()
+            send(over(slot, y_peer, pass_send, pass_recv, core_peer))
+
+    def mean_copy(which, i, peer):
+        view = means.at[quarter(which), :]
+        return remote(view, view, mean_send.at[i], mean_recv.at[i], me, peer)
+
+    def add_grads(slot):
+        if slot == 0:
+            own_copies[4].wait()
+        else:
+            x_copies[slot].wait_recv()
+
+        @pl.loop(0, shard // TILE)
+        def _(tile):
+            at = pl.ds(pl.multiple_of(tile * TILE, TILE), TILE)
+            term = lax.dot_general(
+                rows_in[slot, :, at], cots[slot], (((0,), (0,)), ((), ())),
+                preferred_element_type=jnp.float32,
+            )
+            if slot == 0:
+                grads[at, :] = term
+            else:
+                grads[at, :] += term
+
+    def put_input_grad(slot):
+        over(slot, mine, core_send, core_recv, core_peer).wait_recv()
+        over(slot, y_peer, pass_send, pass_recv, core_peer).wait_recv()
+        base = owner(slot) * shard
+
+        @pl.loop(0, shard // TILE)
+        def _(tile):
+            at = pl.ds(pl.multiple_of(tile * TILE, TILE), TILE)
+            term = lax.dot_general(
+                cots[0], anchors[slot, at, :], (((1,), (1,)), ((), ())),
+                preferred_element_type=jnp.float32,
+            )
+            columns = pl.ds(pl.multiple_of(base + tile * TILE, TILE), TILE)
+            input_grad[:, columns] = (term * scale).astype(input_grad.dtype)
+
+    cot_turn(1)
+
+    for copy in own_copies[1:4]:
+        copy.wait()
+    for copy in pg_copies:
+        copy.wait_recv()
+
+    chunk = 32
+
+    @pl.loop(0, part // chunk)
+    def _(i):
+        at = pl.ds(pl.multiple_of(i * chunk, chunk), chunk)
+        to = pl.ds(pl.multiple_of(mine * part + i * chunk, chunk), chunk)
+        total = pg_own[at, :].astype(jnp.float32)
+        for peer in range(3):
+            total += pg_in[peer, at, :].astype(jnp.float32)
+        mean = total / 4
+        moved = MOMENTUM * moment_own[at, :] + mean
+        updated = anchor_own[at, :].astype(jnp.float32) - OUTER_RATE * (mean + MOMENTUM * moved)
+        anchors[0, to, :] = updated.astype(anchors.dtype)
+        means[to, :] = mean.astype(means.dtype)
+
+    for copy in ring_steps[1]:
+        send(copy)
+    spread(0)
+    send(mean_copy(mine, 0, core_peer))
+    send(mean_copy(mine, 1, y_peer))
+    add_grads(0)
+
+    for step in range(1, half + 1):
+        for copy in ring_steps[step]:
+            copy.wait_recv()
+        if step < half:
+            for copy in ring_steps[step + 1]:
+                send(copy)
+        spread(step)
+        if step < half:
+            cot_turn(step + 1)
+        hand_on(step - 1)
+        if step == 1:
+            mean_copy(mine, 1, y_peer).wait_recv()
+            send(mean_copy(y_peer, 2, core_peer))
+        if step >= 2:
+            for slot in slots_of(step - 2):
+                put_input_grad(slot)
+            for slot in slots_of(step - 1):
+                add_grads(slot)
+
+    for slot in slots_of(half - 1):
+        put_input_grad(slot)
+    mean_copy(mine, 0, core_peer).wait_recv()
+    mean_copy(y_peer, 2, core_peer).wait_recv()
+
+    @pl.loop(0, shard // chunk)
+    def _(i):
+        at = pl.ds(pl.multiple_of(i * chunk, chunk), chunk)
+        mean_out[at, :] = means[at, :]
+
+    for slot in slots_of(half):
+        add_grads(slot)
+    hand_on(half)
+    for slot in slots_of(half):
+        put_input_grad(slot)
+    for copy in sent:
+        copy.wait_send()
+
+
+def exchange(n, scale, pg, anchor, moment, inputs, cot):
+    tokens, width = inputs.shape
+    shard, keys = anchor.shape
+    part = shard // 4
+    bf16, f32 = jnp.bfloat16, jnp.float32
+    sem = pltpu.SemaphoreType.DMA
+    return pl.pallas_call(
+        functools.partial(exchange_kernel, n, scale),
+        out_shape=(
+            jax.ShapeDtypeStruct((shard, keys), f32),
+            jax.ShapeDtypeStruct((shard, keys), bf16),
+            jax.ShapeDtypeStruct((tokens, width), bf16),
+        ),
+        in_specs=[pl.BlockSpec(memory_space=pl.ANY)] * 5,
+        out_specs=(pl.BlockSpec(memory_space=pltpu.VMEM),) * 3,
+        scratch_shapes=[
+            pltpu.VMEM((n, tokens, shard), bf16),
+            pltpu.VMEM((n, tokens, keys), bf16),
+            pltpu.VMEM((n, shard, keys), bf16),
+            pltpu.VMEM((3, part, keys), bf16),
+            pltpu.VMEM((part, keys), bf16),
+            pltpu.VMEM((part, keys), bf16),
+            pltpu.VMEM((part, keys), f32),
+            pltpu.VMEM((shard, keys), bf16),
+            sem((5,)),
+            sem((3,)), sem((3,)),
+            sem((n,)), sem((n,)),
+            sem((n + 1,)), sem((n + 1,)),
+            sem((n + 1,)), sem((n + 1,)),
+            sem((n,)), sem((n,)),
+            sem((n,)), sem((n,)),
+            sem((n,)), sem((n,)),
+            sem((3,)), sem((3,)),
+        ],
+        compiler_params=pltpu.CompilerParams(
+            collective_id=0, has_side_effects=True, vmem_limit_bytes=58 * 2**20
+        ),
+        cost_estimate=pl.CostEstimate(
+            flops=4 * tokens * width * keys,
+            bytes_accessed=2 * (2 * tokens * width + 4 * shard * keys),
+            transcendentals=0,
+        ),
+    )(pg, anchor, moment, inputs, cot)
+
 
 def per_device(anchor, pseudo_grads, outer_moment, adam_first, adam_second, inputs, key_cotangent):
-    width = inputs.shape[1]
-    scale = width ** (-0.5)
-    workers = lax.axis_size("group")
-    total = lax.psum(pseudo_grads[0].astype(jnp.float32).astype(jnp.bfloat16), "group").astype(
-        jnp.float32
+    scale = inputs.shape[1] ** (-0.5)
+    raw, mean, input_grad = exchange(
+        lax.axis_size("fsdp"), scale, pseudo_grads, anchor, outer_moment, inputs, key_cotangent
     )
-    mean_delta = total / workers
+    mean_delta = mean.astype(jnp.float32)
+    grads = raw * scale
     new_moment = MOMENTUM * outer_moment + mean_delta
     new_anchor = (
         anchor.astype(jnp.float32) - OUTER_RATE * (mean_delta + MOMENTUM * new_moment)
     ).astype(jnp.bfloat16)
-    product = jnp.einsum(
-        "tk,dk->td",
-        key_cotangent,
-        lax.all_gather(new_anchor, "fsdp", axis=0, tiled=True),
-        preferred_element_type=jnp.float32,
-    )
-    input_grad = (product * scale).astype(jnp.bfloat16)
-    grads = lax.psum_scatter(
-        (
-            jnp.einsum("td,tk->dk", inputs, key_cotangent, preferred_element_type=jnp.float32)
-            * scale
-        ).astype(jnp.bfloat16),
-        "fsdp",
-        scatter_dimension=0,
-        tiled=True,
-    ).astype(jnp.float32)
     correct_one = 1.0 - BETA_ONE**ADAM_STEP
     correct_two = 1.0 - BETA_TWO**ADAM_STEP
     first_moment = BETA_ONE * adam_first[0] + (1.0 - BETA_ONE) * grads

time: 566 us -> 231 us (0.41)
  the two profiles are of different devices: /device:TPU:0 before, /device:TPU:9 now
where the time goes in v1:
time: 231 us
  Pallas kernels  217 us (94%)
  other arithmetic  11.6 us (5%)
    pallas_call x1, Pallas kernels, exchange(): pl.pallas_call(functools.partial(exchange_kernel, n, scale), out_shape=(j...  217 us
    broadcast_in_dim x1, other arithmetic, per_device(): inner_weights[None]  11.6 us

profile of v1, /device:TPU:9, one launch (start us, length us, event | category | flops | bytes accessed | tf_op | source)
XLA Modules:
  0.0 231.2 jit_solution(5576839568442927550)
XLA Ops:
  0.6 0.0 copy-start
  0.6 216.9 %shard_map.118 = (f32[1024,1024]{1,0:T(8,128)}, bf16[1024,1024]{1,0:T(8,128)(2,1)}, bf16[256,8192]{1,0:T(8,128)(2,1)}) custom-call(bf16[1,1024,1024]{2,1,0:T(8,128)(2,1)} %pg.1, bf16[1024,1024]{1,0:T(8,128)(2,1)} %anchor.1, f32[1024,1024]{1,0:T(8,128)} %moment.1, bf16[256,8192]{1,0:T(8,128)(2,1)} %inputs.1, bf16[256,1024]{1,0:T(8,128)(2,1)} %cot.1), custom_call_target="tpu_custom_call" | custom-call | flops 8589934592 | bytes 16777216 | tf_op jit(solution)/shard_map/pallas_call | solution.py:287
  217.6 0.0 copy-done
  217.6 0.0 copy-start.1
  217.6 11.6 %fusion.3 = (bf16[1,1024,1024]{2,1,0:T(8,128)(2,1)}, bf16[1024,1024]{1,0:T(8,128)(2,1)}, f32[1024,1024]{1,0:T(8,128)}, f32[1,1024,1024]{2,1,0:T(8,128)}, f32[1,1024,1024]{2,1,0:T(8,128)}) fusion(f32[1024,1024]{1,0:T(8,128)} %get-tuple-element.10, f32[1,1024,1024]{2,1,0:T(8,128)} %param.10, f32[1,1024,1024]{2,1,0:T(8,128)} %param.11, ...), kind=kLoop, calls=%fused_computation.8 | loop fusion | flops 27262976 | bytes 37748736 | tf_op jit(solution)/shard_map/broadcast_in_dim | solution.py:348
  229.2 0.0 copy-done.1
  229.2 2.0 copy.14
Async XLA Ops:
  0.6 217.0 %copy-start = (f32[1024,1024]{1,0:T(8,128)S(1)}, f32[1024,1024]{1,0:T(8,128)}, u32[]{:S(2)}) copy-start(f32[1024,1024]{1,0:T(8,128)} %moment.1) | copy-start | bytes 12582916
  217.6 11.6 %copy-start.1 = (bf16[256,8192]{1,0:T(8,128)(2,1)S(1)}, bf16[256,8192]{1,0:T(8,128)(2,1)}, u32[]{:S(2)}) copy-start(bf16[256,8192]{1,0:T(8,128)(2,1)} %get-tuple-element.28) | copy-start | bytes 12582916

commit v2 on v1

--- a/solution.py
+++ b/solution.py
@@ -20,15 +20,22 @@
 MESH = pl.DeviceIdType.MESH
 
 
-def ring_to_index(place, n):
-    back = lax.div(place, n // 2)
-    return (1 - back) * 2 * place + back * (2 * n - 1 - 2 * place)
-
-
-def index_to_ring(index, n):
-    column = lax.rem(index, 2)
-    row = lax.div(index, 2)
-    return (1 - column) * row + column * (n - 1 - row)
+def flip(index, slot):
+    bit = 1
+    while bit <= slot:
+        if slot & bit:
+            index = index + bit * (1 - 2 * lax.rem(lax.div(index, bit), 2))
+        bit *= 2
+    return index
+
+
+def children(slot, n):
+    top = slot & -slot if slot else n
+    return [slot | 1 << at for at in reversed(range(n.bit_length() - 1)) if 1 << at < top]
+
+
+def level_slots(level, n):
+    return [slot for slot in range(n) if bin(slot).count("1") == level]
 
 
 def exchange_kernel(
@@ -37,18 +44,15 @@
     grads, mean_out, input_grad,
     rows_in, cots, anchors, pg_in, pg_own, anchor_own, moment_own, means,
     local_sem,
-    pg_send, pg_recv, x_send, x_recv, cot_send, cot_recv, ring_send, ring_recv,
+    pg_send, pg_recv, x_send, x_recv, cot_send, cot_recv, tree_send, tree_recv,
     y_send, y_recv, core_send, core_recv, pass_send, pass_recv, mean_send, mean_recv,
 ):
-    half = n // 2
+    levels = n.bit_length() - 1
     tokens = inputs.shape[0]
     shard = anchor.shape[0]
     part = shard // 4
     me = lax.axis_index("fsdp")
     mine = lax.axis_index("group")
-    place = index_to_ring(me, n)
-    right = ring_to_index(lax.rem(place + 1, n), n)
-    left = ring_to_index(lax.rem(place + n - 1, n), n)
     y, core = lax.div(mine, 2), lax.rem(mine, 2)
     core_peer = 2 * y + 1 - core
     y_peer = 2 * (1 - y) + core
@@ -56,7 +60,7 @@
     peers = (core_peer, y_peer, far_peer)
 
     def owner(slot):
-        return ring_to_index(lax.rem(place + n - slot, n), n)
+        return flip(me, slot)
 
     def quarter(which):
         return pl.ds(pl.multiple_of(which * part, part), part)
@@ -107,70 +111,53 @@
     for i in (1, 2, 0):
         send(pg_copies[i])
 
-    def ring_step(buffer, rows, first, step, send_sem, recv_sem):
-        if step < half:
-            spans = ((first, rows, step), (first, rows, n - step))
-        else:
-            spans = ((first, rows // 2, half), (first + rows // 2, rows // 2, n))
-        (up, up_rows, up_sem), (down, down_rows, down_sem) = spans
-        up_at = pl.ds(pl.multiple_of(up, rows // 2), up_rows)
-        down_at = pl.ds(pl.multiple_of(down, rows // 2), down_rows)
-        return (
-            remote(
-                buffer.at[step - 1, up_at, :], buffer.at[step, up_at, :],
-                send_sem.at[up_sem], recv_sem.at[up_sem], right, mine,
-            ),
-            remote(
-                buffer.at[(n - step + 1) % n, down_at, :], buffer.at[n - step, down_at, :],
-                send_sem.at[down_sem], recv_sem.at[down_sem], left, mine,
-            ),
-        )
-
-    cot_steps = [None] + [
-        ring_step(cots, tokens, 0, step, cot_send, cot_recv) for step in range(1, half + 1)
-    ]
-    ring_steps = [None] + [
-        ring_step(anchors, part, mine * part, step, ring_send, ring_recv)
-        for step in range(1, half + 1)
-    ]
+    def tree_copy(buffer, rows, slot, child, send_sem, recv_sem):
+        return remote(
+            buffer.at[slot, rows, :], buffer.at[child, rows, :],
+            send_sem.at[child], recv_sem.at[child], flip(me, child - slot), mine,
+        )
+
+    def parent(slot):
+        return slot & (slot - 1)
+
+    def cot_copy(child):
+        return tree_copy(cots, pl.ds(0, tokens), parent(child), child, cot_send, cot_recv)
+
+    def anchor_copy(child):
+        return tree_copy(anchors, quarter(mine), parent(child), child, tree_send, tree_recv)
 
     own_copies[0].wait()
-    for copy in cot_steps[1]:
-        send(copy)
-
-    x_copies = [None] * n
-    for step in range(1, half + 1):
-        for slot in (step, n - step) if step < half else (half,):
-            target = ring_to_index(lax.rem(place + slot, n), n)
-            x_copies[slot] = remote(
-                inputs.at[:, shard_columns(target)], rows_in.at[slot],
-                x_send.at[slot], x_recv.at[slot], target, mine,
-            )
-            send(x_copies[slot])
-
-    def cot_turn(step):
-        for copy in cot_steps[step]:
-            copy.wait_recv()
-        if step < half:
-            for copy in cot_steps[step + 1]:
-                send(copy)
-
-    def slots_of(step):
-        if step == 0:
-            return (0,)
-        return (step, n - step) if step < half else (half,)
+    for child in children(0, n):
+        send(cot_copy(child))
+
+    def x_copy(slot):
+        target = owner(slot)
+        return remote(
+            inputs.at[:, shard_columns(target)], rows_in.at[slot],
+            x_send.at[slot], x_recv.at[slot], target, mine,
+        )
+
+    order = sorted(range(1, n), reverse=True)
+    early = [slot for slot in order if bin(slot).count("1") < 2 or slot == n // 2 + 1]
+    for slot in early:
+        send(x_copy(slot))
+
+    def cot_turn(level):
+        for slot in level_slots(level, n):
+            cot_copy(slot).wait_recv()
+            for child in children(slot, n):
+                send(cot_copy(child))
 
     def over(slot, which, send_sem, recv_sem, peer):
         view = anchors.at[slot, quarter(which), :]
         return remote(view, view, send_sem.at[slot], recv_sem.at[slot], me, peer)
 
-    def spread(step):
-        for slot in slots_of(step):
-            send(over(slot, mine, y_send, y_recv, y_peer))
-            send(over(slot, mine, core_send, core_recv, core_peer))
-
-    def hand_on(step):
-        for slot in slots_of(step):
+    def spread(slot):
+        send(over(slot, mine, y_send, y_recv, y_peer))
+        send(over(slot, mine, core_send, core_recv, core_peer))
+
+    def hand_on(level):
+        for slot in level_slots(level, n):
             over(slot, mine, y_send, y_recv, y_peer).wait_recv()
             send(over(slot, y_peer, pass_send, pass_recv, core_peer))
 
@@ -182,7 +169,7 @@
         if slot == 0:
             own_copies[4].wait()
         else:
-            x_copies[slot].wait_recv()
+            x_copy(slot).wait_recv()
 
         @pl.loop(0, shard // TILE)
         def _(tile):
@@ -210,8 +197,6 @@
             )
             columns = pl.ds(pl.multiple_of(base + tile * TILE, TILE), TILE)
             input_grad[:, columns] = (term * scale).astype(input_grad.dtype)
-
-    cot_turn(1)
 
     for copy in own_copies[1:4]:
         copy.wait()
@@ -233,33 +218,42 @@
         anchors[0, to, :] = updated.astype(anchors.dtype)
         means[to, :] = mean.astype(means.dtype)
 
-    for copy in ring_steps[1]:
-        send(copy)
+    for child in children(0, n):
+        send(anchor_copy(child))
     spread(0)
-    send(mean_copy(mine, 0, core_peer))
-    send(mean_copy(mine, 1, y_peer))
-    add_grads(0)
-
-    for step in range(1, half + 1):
-        for copy in ring_steps[step]:
-            copy.wait_recv()
-        if step < half:
-            for copy in ring_steps[step + 1]:
-                send(copy)
-        spread(step)
-        if step < half:
-            cot_turn(step + 1)
-        hand_on(step - 1)
-        if step == 1:
+    cot_turn(1)
+
+    for level in range(1, levels + 1):
+        for slot in level_slots(level, n):
+            anchor_copy(slot).wait_recv()
+            for child in children(slot, n):
+                send(anchor_copy(child))
+            spread(slot)
+        if level == 1:
+            for slot in order:
+                if slot not in early:
+                    send(x_copy(slot))
+            send(mean_copy(mine, 0, core_peer))
+            send(mean_copy(mine, 1, y_peer))
+        if level < levels:
+            cot_turn(level + 1)
+        hand_on(level - 1)
+        if level == 1:
+            add_grads(0)
+        if level == 2:
             mean_copy(mine, 1, y_peer).wait_recv()
             send(mean_copy(y_peer, 2, core_peer))
-        if step >= 2:
-            for slot in slots_of(step - 2):
+        if level >= 2:
+            for slot in level_slots(level - 2, n):
                 put_input_grad(slot)
-            for slot in slots_of(step - 1):
+        if level == 2:
+            for slot in level_slots(1, n)[:2]:
                 add_grads(slot)
 
-    for slot in slots_of(half - 1):
+    late = [slot for slot in range(1, n) if slot not in level_slots(1, n)[:2]]
+    for slot in late[: len(late) // 2]:
+        add_grads(slot)
+    for slot in level_slots(levels - 1, n):
         put_input_grad(slot)
     mean_copy(mine, 0, core_peer).wait_recv()
     mean_copy(y_peer, 2, core_peer).wait_recv()
@@ -269,11 +263,10 @@
         at = pl.ds(pl.multiple_of(i * chunk, chunk), chunk)
         mean_out[at, :] = means[at, :]
 
-    for slot in slots_of(half):
+    hand_on(levels)
+    for slot in late[len(late) // 2 :]:
         add_grads(slot)
-    hand_on(half)
-    for slot in slots_of(half):
-        put_input_grad(slot)
+    put_input_grad(n - 1)
     for copy in sent:
         copy.wait_send()
 
@@ -305,8 +298,8 @@
             sem((5,)),
             sem((3,)), sem((3,)),
             sem((n,)), sem((n,)),
-            sem((n + 1,)), sem((n + 1,)),
-            sem((n + 1,)), sem((n + 1,)),
+            sem((n,)), sem((n,)),
+            sem((n,)), sem((n,)),
             sem((n,)), sem((n,)),
             sem((n,)), sem((n,)),
             sem((n,)), sem((n,)),

time: 231 us -> 192 us (0.83)
  the two profiles are of different devices: /device:TPU:9 before, /device:TPU:0 now
where the time goes in v2:
time: 192 us
  Pallas kernels  178 us (93%)
  other arithmetic  11.6 us (6%)
  local copies, waits for them, and re-layouts  2.02 us (1%)
    pallas_call x1, Pallas kernels, exchange(): pl.pallas_call(functools.partial(exchange_kernel, n, scale), out_shape=(j...  178 us
    broadcast_in_dim x1, other arithmetic, per_device(): inner_weights[None]  11.6 us

profile of v2, /device:TPU:0, one launch (start us, length us, event | category | flops | bytes accessed | tf_op | source)
XLA Modules:
  0.0 192.1 jit_solution(6987103420323277419)
XLA Ops:
  0.6 0.0 copy-start
  0.6 177.8 %shard_map.118 = (f32[1024,1024]{1,0:T(8,128)}, bf16[1024,1024]{1,0:T(8,128)(2,1)}, bf16[256,8192]{1,0:T(8,128)(2,1)}) custom-call(bf16[1,1024,1024]{2,1,0:T(8,128)(2,1)} %pg.1, bf16[1024,1024]{1,0:T(8,128)(2,1)} %anchor.1, f32[1024,1024]{1,0:T(8,128)} %moment.1, bf16[256,8192]{1,0:T(8,128)(2,1)} %inputs.1, bf16[256,1024]{1,0:T(8,128)(2,1)} %cot.1), custom_call_target="tpu_custom_call" | custom-call | flops 8589934592 | bytes 16777216 | tf_op jit(solution)/shard_map/pallas_call | solution.py:280
  178.5 0.0 copy-done
  178.5 0.0 copy-start.1
  178.5 11.6 %fusion.3 = (bf16[1,1024,1024]{2,1,0:T(8,128)(2,1)}, bf16[1024,1024]{1,0:T(8,128)(2,1)}, f32[1024,1024]{1,0:T(8,128)}, f32[1,1024,1024]{2,1,0:T(8,128)}, f32[1,1024,1024]{2,1,0:T(8,128)}) fusion(f32[1024,1024]{1,0:T(8,128)} %get-tuple-element.10, f32[1,1024,1024]{2,1,0:T(8,128)} %param.10, f32[1,1024,1024]{2,1,0:T(8,128)} %param.11, ...), kind=kLoop, calls=%fused_computation.8 | loop fusion | flops 27262976 | bytes 37748736 | tf_op jit(solution)/shard_map/broadcast_in_dim | solution.py:341
  190.1 0.0 copy-done.1
  190.1 2.0 %copy.14 = bf16[256,8192]{1,0:T(8,128)(2,1)} copy(bf16[256,8192]{1,0:T(8,128)(2,1)S(1)} %copy-done.1) | data formatting | bytes 8388608
Async XLA Ops:
  0.6 177.8 %copy-start = (f32[1024,1024]{1,0:T(8,128)S(1)}, f32[1024,1024]{1,0:T(8,128)}, u32[]{:S(2)}) copy-start(f32[1024,1024]{1,0:T(8,128)} %moment.1) | copy-start | bytes 12582916
  178.5 11.6 %copy-start.1 = (bf16[256,8192]{1,0:T(8,128)(2,1)S(1)}, bf16[256,8192]{1,0:T(8,128)(2,1)}, u32[]{:S(2)}) copy-start(bf16[256,8192]{1,0:T(8,128)(2,1)} %get-tuple-element.28) | copy-start | bytes 12582916

commit v3 on v2

--- a/solution.py
+++ b/solution.py
@@ -17,6 +17,7 @@
 ADAM_STEP = 100
 
 TILE = 256
+PIECES = 2
 MESH = pl.DeviceIdType.MESH
 
 
@@ -41,9 +42,10 @@
 def exchange_kernel(
     n, scale,
     pg, anchor, moment, inputs, cot,
-    grads, mean_out, input_grad,
-    rows_in, cots, anchors, pg_in, pg_own, anchor_own, moment_own, means,
-    local_sem,
+    grads_out, mean_out, input_grad_out,
+    grads, input_grad,
+    rows_in, cots, anchors, pg_core, pg_y, pg_pair, pg_own, anchor_own, moment_own, means,
+    local_sem, out_sem,
     pg_send, pg_recv, x_send, x_recv, cot_send, cot_recv, tree_send, tree_recv,
     y_send, y_recv, core_send, core_recv, pass_send, pass_recv, mean_send, mean_recv,
 ):
@@ -56,14 +58,18 @@
     y, core = lax.div(mine, 2), lax.rem(mine, 2)
     core_peer = 2 * y + 1 - core
     y_peer = 2 * (1 - y) + core
-    far_peer = 2 * (1 - y) + 1 - core
-    peers = (core_peer, y_peer, far_peer)
+    piece_rows = part // PIECES
 
     def owner(slot):
         return flip(me, slot)
 
     def quarter(which):
         return pl.ds(pl.multiple_of(which * part, part), part)
+
+    def piece_of(which, piece):
+        return pl.ds(
+            pl.multiple_of(which * part + piece * piece_rows, piece_rows), piece_rows
+        )
 
     def local(src, dst, sem):
         return pltpu.make_async_copy(src, dst, local_sem.at[sem])
@@ -79,10 +85,11 @@
 
     own_copies = [
         local(cot, cots.at[0], 0),
-        local(pg.at[0, quarter(mine), :], pg_own, 1),
-        local(anchor.at[quarter(mine), :], anchor_own, 2),
-        local(moment.at[quarter(mine), :], moment_own, 3),
-        local(inputs.at[:, shard_columns(me)], rows_in.at[0], 4),
+        local(pg.at[0, quarter(mine), :], pg_own.at[0], 1),
+        local(pg.at[0, quarter(y_peer), :], pg_own.at[1], 2),
+        local(anchor.at[quarter(mine), :], anchor_own, 3),
+        local(moment.at[quarter(mine), :], moment_own, 4),
+        local(inputs.at[:, shard_columns(me)], rows_in.at[0], 5),
     ]
     for copy in own_copies:
         copy.start()
@@ -92,11 +99,11 @@
         pl.semaphore_signal(
             barrier, inc=1, device_id={"group": mine, "fsdp": owner(step)}, device_id_type=MESH
         )
-    for peer in peers:
+    for peer in (core_peer, y_peer):
         pl.semaphore_signal(
             barrier, inc=1, device_id={"group": peer, "fsdp": me}, device_id_type=MESH
         )
-    pl.semaphore_wait(barrier, n + 2)
+    pl.semaphore_wait(barrier, n + 1)
 
     sent = []
 
@@ -104,11 +111,15 @@
         copy.start()
         sent.append(copy)
 
-    pg_copies = [
-        remote(pg.at[0, quarter(peer), :], pg_in.at[i], pg_send.at[i], pg_recv.at[i], me, peer)
-        for i, peer in enumerate(peers)
-    ]
-    for i in (1, 2, 0):
+    def pg_core_copy(i, theirs):
+        return remote(
+            pg.at[0, quarter(theirs), :], pg_core.at[i], pg_send.at[i], pg_recv.at[i],
+            me, core_peer,
+        )
+
+    core_of_y = 2 * (1 - y) + 1 - core
+    pg_copies = [pg_core_copy(0, core_peer), pg_core_copy(1, core_of_y)]
+    for i in (1, 0):
         send(pg_copies[i])
 
     def tree_copy(buffer, rows, slot, child, send_sem, recv_sem):
@@ -123,8 +134,11 @@
     def cot_copy(child):
         return tree_copy(cots, pl.ds(0, tokens), parent(child), child, cot_send, cot_recv)
 
-    def anchor_copy(child):
-        return tree_copy(anchors, quarter(mine), parent(child), child, tree_send, tree_recv)
+    def anchor_copy(child, piece):
+        return tree_copy(
+            anchors, piece_of(mine, piece), parent(child), child,
+            tree_send.at[piece], tree_recv.at[piece],
+        )
 
     own_copies[0].wait()
     for child in children(0, n):
@@ -137,10 +151,30 @@
             x_send.at[slot], x_recv.at[slot], target, mine,
         )
 
-    order = sorted(range(1, n), reverse=True)
-    early = [slot for slot in order if bin(slot).count("1") < 2 or slot == n // 2 + 1]
-    for slot in early:
-        send(x_copy(slot))
+    bulk = {
+        0: level_slots(1, n)[::-1],
+        1: [slot for slot in level_slots(2, n)[::-1] if slot >= n // 2],
+    }
+    bulk[2] = [slot for slot in range(n - 1, 0, -1) if slot not in bulk[0] + bulk[1]]
+
+    def send_bulk(turn):
+        for slot in bulk[turn]:
+            send(x_copy(slot))
+
+    chunk = 32
+
+    own_copies[2].wait()
+    pg_copies[1].wait_recv()
+
+    @pl.loop(0, part // chunk)
+    def _(i):
+        at = pl.ds(pl.multiple_of(i * chunk, chunk), chunk)
+        pair = pg_own[1, at, :].astype(jnp.float32) + pg_core[1, at, :].astype(jnp.float32)
+        pg_pair[at, :] = pair.astype(pg_pair.dtype)
+
+    pg_y_copy = remote(pg_pair, pg_y, pg_send.at[2], pg_recv.at[2], me, y_peer)
+    send(pg_y_copy)
+    send_bulk(0)
 
     def cot_turn(level):
         for slot in level_slots(level, n):
@@ -148,26 +182,34 @@
             for child in children(slot, n):
                 send(cot_copy(child))
 
-    def over(slot, which, send_sem, recv_sem, peer):
-        view = anchors.at[slot, quarter(which), :]
-        return remote(view, view, send_sem.at[slot], recv_sem.at[slot], me, peer)
-
-    def spread(slot):
-        send(over(slot, mine, y_send, y_recv, y_peer))
-        send(over(slot, mine, core_send, core_recv, core_peer))
+    def over(slot, piece, which, send_sem, recv_sem, peer):
+        view = anchors.at[slot, piece_of(which, piece), :]
+        return remote(view, view, send_sem.at[piece, slot], recv_sem.at[piece, slot], me, peer)
+
+    def spread(slot, piece):
+        send(over(slot, piece, mine, y_send, y_recv, y_peer))
+        send(over(slot, piece, mine, core_send, core_recv, core_peer))
 
     def hand_on(level):
-        for slot in level_slots(level, n):
-            over(slot, mine, y_send, y_recv, y_peer).wait_recv()
-            send(over(slot, y_peer, pass_send, pass_recv, core_peer))
+        for piece in range(PIECES):
+            for slot in level_slots(level, n):
+                over(slot, piece, mine, y_send, y_recv, y_peer).wait_recv()
+                send(over(slot, piece, y_peer, pass_send, pass_recv, core_peer))
 
     def mean_copy(which, i, peer):
         view = means.at[quarter(which), :]
         return remote(view, view, mean_send.at[i], mean_recv.at[i], me, peer)
 
+    out_copies = []
+
+    def put_out(src, dst, at):
+        copy = pltpu.make_async_copy(src, dst, out_sem.at[at])
+        copy.start()
+        out_copies.append(copy)
+
     def add_grads(slot):
         if slot == 0:
-            own_copies[4].wait()
+            own_copies[5].wait()
         else:
             x_copy(slot).wait_recv()
 
@@ -184,8 +226,9 @@
                 grads[at, :] += term
 
     def put_input_grad(slot):
-        over(slot, mine, core_send, core_recv, core_peer).wait_recv()
-        over(slot, y_peer, pass_send, pass_recv, core_peer).wait_recv()
+        for piece in range(PIECES):
+            over(slot, piece, mine, core_send, core_recv, core_peer).wait_recv()
+            over(slot, piece, y_peer, pass_send, pass_recv, core_peer).wait_recv()
         base = owner(slot) * shard
 
         @pl.loop(0, shard // TILE)
@@ -198,77 +241,77 @@
             columns = pl.ds(pl.multiple_of(base + tile * TILE, TILE), TILE)
             input_grad[:, columns] = (term * scale).astype(input_grad.dtype)
 
-    for copy in own_copies[1:4]:
-        copy.wait()
-    for copy in pg_copies:
-        copy.wait_recv()
-
-    chunk = 32
+        put_out(
+            input_grad.at[:, shard_columns(owner(slot))],
+            input_grad_out.at[:, shard_columns(owner(slot))], slot,
+        )
+
+    for at in (1, 3, 4):
+        own_copies[at].wait()
+    pg_copies[0].wait_recv()
+    pg_y_copy.wait_recv()
 
     @pl.loop(0, part // chunk)
     def _(i):
         at = pl.ds(pl.multiple_of(i * chunk, chunk), chunk)
         to = pl.ds(pl.multiple_of(mine * part + i * chunk, chunk), chunk)
-        total = pg_own[at, :].astype(jnp.float32)
-        for peer in range(3):
-            total += pg_in[peer, at, :].astype(jnp.float32)
-        mean = total / 4
+        total = pg_own[0, at, :].astype(jnp.float32) + pg_core[0, at, :].astype(jnp.float32)
+        mean = (total + pg_y[at, :].astype(jnp.float32)) / 4
         moved = MOMENTUM * moment_own[at, :] + mean
         updated = anchor_own[at, :].astype(jnp.float32) - OUTER_RATE * (mean + MOMENTUM * moved)
         anchors[0, to, :] = updated.astype(anchors.dtype)
         means[to, :] = mean.astype(means.dtype)
 
-    for child in children(0, n):
-        send(anchor_copy(child))
-    spread(0)
+    for piece in range(PIECES):
+        for child in children(0, n):
+            send(anchor_copy(child, piece))
+        spread(0, piece)
+    send(mean_copy(mine, 0, core_peer))
+    send(mean_copy(mine, 1, y_peer))
     cot_turn(1)
 
+    late = level_slots(1, n)
     for level in range(1, levels + 1):
-        for slot in level_slots(level, n):
-            anchor_copy(slot).wait_recv()
-            for child in children(slot, n):
-                send(anchor_copy(child))
-            spread(slot)
-        if level == 1:
-            for slot in order:
-                if slot not in early:
-                    send(x_copy(slot))
-            send(mean_copy(mine, 0, core_peer))
-            send(mean_copy(mine, 1, y_peer))
+        for piece in range(PIECES):
+            for slot in level_slots(level, n):
+                anchor_copy(slot, piece).wait_recv()
+                for child in children(slot, n):
+                    send(anchor_copy(child, piece))
+                spread(slot, piece)
+        if level < 3:
+            send_bulk(level)
         if level < levels:
             cot_turn(level + 1)
         hand_on(level - 1)
         if level == 1:
             add_grads(0)
-        if level == 2:
             mean_copy(mine, 1, y_peer).wait_recv()
             send(mean_copy(y_peer, 2, core_peer))
         if level >= 2:
             for slot in level_slots(level - 2, n):
                 put_input_grad(slot)
         if level == 2:
-            for slot in level_slots(1, n)[:2]:
+            for slot in late[:-1]:
                 add_grads(slot)
-
-    late = [slot for slot in range(1, n) if slot not in level_slots(1, n)[:2]]
-    for slot in late[: len(late) // 2]:
+        if level == 3:
+            add_grads(late[-1])
+
+    mean_copy(mine, 0, core_peer).wait_recv()
+    mean_copy(y_peer, 2, core_peer).wait_recv()
+    put_out(means, mean_out, n)
+    for slot in bulk[1]:
         add_grads(slot)
     for slot in level_slots(levels - 1, n):
         put_input_grad(slot)
-    mean_copy(mine, 0, core_peer).wait_recv()
-    mean_copy(y_peer, 2, core_peer).wait_recv()
-
-    @pl.loop(0, shard // chunk)
-    def _(i):
-        at = pl.ds(pl.multiple_of(i * chunk, chunk), chunk)
-        mean_out[at, :] = means[at, :]
-
     hand_on(levels)
-    for slot in late[len(late) // 2 :]:
+    for slot in bulk[2][::-1]:
         add_grads(slot)
+    put_out(grads, grads_out, n + 1)
     put_input_grad(n - 1)
     for copy in sent:
         copy.wait_send()
+    for copy in out_copies:
+        copy.wait()
 
 
 def exchange(n, scale, pg, anchor, moment, inputs, cot):
@@ -285,24 +328,28 @@
             jax.ShapeDtypeStruct((tokens, width), bf16),
         ),
         in_specs=[pl.BlockSpec(memory_space=pl.ANY)] * 5,
-        out_specs=(pl.BlockSpec(memory_space=pltpu.VMEM),) * 3,
+        out_specs=(pl.BlockSpec(memory_space=pl.ANY),) * 3,
         scratch_shapes=[
+            pltpu.VMEM((shard, keys), f32),
+            pltpu.VMEM((tokens, width), bf16),
             pltpu.VMEM((n, tokens, shard), bf16),
             pltpu.VMEM((n, tokens, keys), bf16),
             pltpu.VMEM((n, shard, keys), bf16),
-            pltpu.VMEM((3, part, keys), bf16),
+            pltpu.VMEM((2, part, keys), bf16),
             pltpu.VMEM((part, keys), bf16),
+            pltpu.VMEM((part, keys), bf16),
+            pltpu.VMEM((2, part, keys), bf16),
             pltpu.VMEM((part, keys), bf16),
             pltpu.VMEM((part, keys), f32),
             pltpu.VMEM((shard, keys), bf16),
-            sem((5,)),
+            sem((6,)), sem((n + 2,)),
             sem((3,)), sem((3,)),
             sem((n,)), sem((n,)),
             sem((n,)), sem((n,)),
-            sem((n,)), sem((n,)),
-            sem((n,)), sem((n,)),
-            sem((n,)), sem((n,)),
-            sem((n,)), sem((n,)),
+            sem((PIECES, n)), sem((PIECES, n)),
+            sem((PIECES, n)), sem((PIECES, n)),
+            sem((PIECES, n)), sem((PIECES, n)),
+            sem((PIECES, n)), sem((PIECES, n)),
             sem((3,)), sem((3,)),
         ],
         compiler_params=pltpu.CompilerParams(

time: 192 us -> 182 us (0.948)
  Pallas kernels: 178 us -> 168 us
    pallas_call x1, Pallas kernels: 178 us -> 168 us  [exchange(): pl.pallas_call(functools.partial(exchange_kernel, n, scale), out_shape=(j...]
where the time goes in v3:
time: 182 us
  Pallas kernels  168 us (92%)
  other arithmetic  11.6 us (6%)
  local copies, waits for them, and re-layouts  2.02 us (1%)
    pallas_call x1, Pallas kernels, exchange(): pl.pallas_call(functools.partial(exchange_kernel, n, scale), out_shape=(j...  168 us
    broadcast_in_dim x1, other arithmetic, per_device(): inner_weights[None]  11.6 us

profile of v3, /device:TPU:0, one launch (start us, length us, event | category | flops | bytes accessed | tf_op | source)
XLA Modules:
  0.0 182.1 jit_solution(4231435510118361341)
XLA Ops:
  0.6 0.0 copy-start
  0.6 167.8 %shard_map.118 = (f32[1024,1024]{1,0:T(8,128)}, bf16[1024,1024]{1,0:T(8,128)(2,1)}, bf16[256,8192]{1,0:T(8,128)(2,1)}) custom-call(bf16[1,1024,1024]{2,1,0:T(8,128)(2,1)} %pg.1, bf16[1024,1024]{1,0:T(8,128)(2,1)} %anchor.1, f32[1024,1024]{1,0:T(8,128)} %moment.1, bf16[256,8192]{1,0:T(8,128)(2,1)} %inputs.1, bf16[256,1024]{1,0:T(8,128)(2,1)} %cot.1), custom_call_target="tpu_custom_call" | custom-call | flops 8589934592 | bytes 16777216 | tf_op jit(solution)/shard_map/pallas_call | solution.py:323
  168.5 0.0 copy-done
  168.5 0.0 copy-start.1
  168.5 11.6 %fusion.3 = (bf16[1,1024,1024]{2,1,0:T(8,128)(2,1)}, bf16[1024,1024]{1,0:T(8,128)(2,1)}, f32[1024,1024]{1,0:T(8,128)}, f32[1,1024,1024]{2,1,0:T(8,128)}, f32[1,1024,1024]{2,1,0:T(8,128)}) fusion(f32[1024,1024]{1,0:T(8,128)} %get-tuple-element.10, f32[1,1024,1024]{2,1,0:T(8,128)} %param.10, f32[1,1024,1024]{2,1,0:T(8,128)} %param.11, ...), kind=kLoop, calls=%fused_computation.8 | loop fusion | flops 27262976 | bytes 37748736 | tf_op jit(solution)/shard_map/broadcast_in_dim | solution.py:388
  180.1 0.0 copy-done.1
  180.1 2.0 %copy.14 = bf16[256,8192]{1,0:T(8,128)(2,1)} copy(bf16[256,8192]{1,0:T(8,128)(2,1)S(1)} %copy-done.1) | data formatting | bytes 8388608
Async XLA Ops:
  0.6 167.8 %copy-start = (f32[1024,1024]{1,0:T(8,128)S(1)}, f32[1024,1024]{1,0:T(8,128)}, u32[]{:S(2)}) copy-start(f32[1024,1024]{1,0:T(8,128)} %moment.1) | copy-start | bytes 12582916
  168.5 11.6 %copy-start.1 = (bf16[256,8192]{1,0:T(8,128)(2,1)S(1)}, bf16[256,8192]{1,0:T(8,128)(2,1)}, u32[]{:S(2)}) copy-start(bf16[256,8192]{1,0:T(8,128)(2,1)} %get-tuple-element.28) | copy-start | bytes 12582916

commit v4 on v3

--- a/solution.py
+++ b/solution.py
@@ -152,9 +152,9 @@
         )
 
     bulk = {
-        0: level_slots(1, n)[::-1],
-        1: [slot for slot in level_slots(2, n)[::-1] if slot >= n // 2],
+        0: [n // 2 + n // 4] + [slot for slot in level_slots(1, n)[::-1] if slot < n // 2],
     }
+    bulk[1] = [slot for slot in range(n - 1, n // 2, -1) if slot not in bulk[0]]
     bulk[2] = [slot for slot in range(n - 1, 0, -1) if slot not in bulk[0] + bulk[1]]
 
     def send_bulk(turn):
@@ -270,7 +270,7 @@
     send(mean_copy(mine, 1, y_peer))
     cot_turn(1)
 
-    late = level_slots(1, n)
+    late = bulk[0][::-1]
     for level in range(1, levels + 1):
         for piece in range(PIECES):
             for slot in level_slots(level, n):
@@ -303,9 +303,10 @@
         add_grads(slot)
     for slot in level_slots(levels - 1, n):
         put_input_grad(slot)
+    for slot in bulk[2][:0:-1]:
+        add_grads(slot)
     hand_on(levels)
-    for slot in bulk[2][::-1]:
-        add_grads(slot)
+    add_grads(bulk[2][0])
     put_out(grads, grads_out, n + 1)
     put_input_grad(n - 1)
     for copy in sent:
@@ -353,7 +354,7 @@
             sem((3,)), sem((3,)),
         ],
         compiler_params=pltpu.CompilerParams(
-            collective_id=0, has_side_effects=True, vmem_limit_bytes=58 * 2**20
+            collective_id=0, has_side_effects=True, vmem_limit_bytes=51 * 2**20
         ),
         cost_estimate=pl.CostEstimate(
             flops=4 * tokens * width * keys,

time: 182 us -> 176 us (0.967)
  Pallas kernels: 168 us -> 162 us
    pallas_call x1, Pallas kernels: 168 us -> 162 us  [exchange(): pl.pallas_call(functools.partial(exchange_kernel, n, scale), out_shape=(j...]
where the time goes in v4:
time: 176 us
  Pallas kernels  162 us (92%)
  other arithmetic  10.2 us (6%)
  local copies, waits for them, and re-layouts  3.07 us (2%)
    pallas_call x1, Pallas kernels, exchange(): pl.pallas_call(functools.partial(exchange_kernel, n, scale), out_shape=(j...  162 us
    broadcast_in_dim x1, other arithmetic, per_device(): inner_weights[None]  10.2 us

profile of v4, /device:TPU:0, one launch (start us, length us, event | category | flops | bytes accessed | tf_op | source)
XLA Modules:
  0.0 175.6 jit_solution(7292135952971163722)
XLA Ops:
  0.6 0.0 copy-start
  0.6 1.0 copy-done
  1.7 0.0 copy-start.1
  1.7 0.0 copy-start.2
  1.7 0.0 copy-start.4
  1.7 161.6 %shard_map.118 = (f32[1024,1024]{1,0:T(8,128)}, bf16[1024,1024]{1,0:T(8,128)(2,1)S(1)}, bf16[256,8192]{1,0:T(8,128)(2,1)}) custom-call(bf16[1,1024,1024]{2,1,0:T(8,128)(2,1)} %pg.1, bf16[1024,1024]{1,0:T(8,128)(2,1)} %anchor.1, f32[1024,1024]{1,0:T(8,128)} %moment.1, bf16[256,8192]{1,0:T(8,128)(2,1)} %inputs.1, bf16[256,1024]{1,0:T(8,128)(2,1)S(1)} %copy-done), custom_call_target="tpu_custom_call" | custom-call | flops 8589934592 | bytes 16777216 | tf_op jit(solution)/shard_map/pallas_call | solution.py:324
  163.3 0.0 copy-done.1
  163.3 0.0 copy-done.2
  163.3 0.0 copy-done.4
  163.3 0.0 copy-start.3
  163.3 10.2 %fusion.3 = (bf16[1,1024,1024]{2,1,0:T(8,128)(2,1)}, bf16[1024,1024]{1,0:T(8,128)(2,1)}, f32[1024,1024]{1,0:T(8,128)}, f32[1,1024,1024]{2,1,0:T(8,128)}, f32[1,1024,1024]{2,1,0:T(8,128)}) fusion(f32[1024,1024]{1,0:T(8,128)} %get-tuple-element.10, f32[1,1024,1024]{2,1,0:T(8,128)S(1)} %copy-done.2, f32[1,1024,1024]{2,1,0:T(8,128)} %param.11, ...), kind=kLoop, calls=%fused_computation.8 | loop fusion | flops 27262976 | bytes 37748736 | tf_op jit(solution)/shard_map/broadcast_in_dim | solution.py:389
  173.5 0.0 copy-done.3
  173.5 2.0 %copy.14 = bf16[256,8192]{1,0:T(8,128)(2,1)} copy(bf16[256,8192]{1,0:T(8,128)(2,1)S(1)} %copy-done.3) | data formatting | bytes 8388608
Async XLA Ops:
  0.6 1.0 copy-start
  1.7 161.6 %copy-start.1 = (f32[1024,1024]{1,0:T(8,128)S(1)}, f32[1024,1024]{1,0:T(8,128)}, u32[]{:S(2)}) copy-start(f32[1024,1024]{1,0:T(8,128)} %moment.1) | copy-start | bytes 12582916
  1.7 161.6 %copy-start.2 = (f32[1,1024,1024]{2,1,0:T(8,128)S(1)}, f32[1,1024,1024]{2,1,0:T(8,128)}, u32[]{:S(2)}) copy-start(f32[1,1024,1024]{2,1,0:T(8,128)} %param.10) | copy-start | bytes 12582916
  1.7 161.6 %copy-start.4 = (bf16[1024,1024]{1,0:T(8,128)(2,1)S(1)}, bf16[1024,1024]{1,0:T(8,128)(2,1)}, u32[]{:S(2)}) copy-start(bf16[1024,1024]{1,0:T(8,128)(2,1)} %anchor.1) | copy-start | bytes 6291460
  163.3 10.2 %copy-start.3 = (bf16[256,8192]{1,0:T(8,128)(2,1)S(1)}, bf16[256,8192]{1,0:T(8,128)(2,1)}, u32[]{:S(2)}) copy-start(bf16[256,8192]{1,0:T(8,128)(2,1)} %get-tuple-element.28) | copy-start | bytes 12582916

commit v5 on v4

--- a/solution.py
+++ b/solution.py
@@ -157,8 +157,13 @@
     bulk[1] = [slot for slot in range(n - 1, n // 2, -1) if slot not in bulk[0]]
     bulk[2] = [slot for slot in range(n - 1, 0, -1) if slot not in bulk[0] + bulk[1]]
 
+    turns = (
+        bulk[0][:1] + bulk[1][:1] + bulk[0][1:],
+        bulk[1][1:] + bulk[2],
+    )
+
     def send_bulk(turn):
-        for slot in bulk[turn]:
+        for slot in turns[turn]:
             send(x_copy(slot))
 
     chunk = 32
@@ -278,8 +283,8 @@
                 for child in children(slot, n):
                     send(anchor_copy(child, piece))
                 spread(slot, piece)
-        if level < 3:
-            send_bulk(level)
+        if level == 1:
+            send_bulk(1)
         if level < levels:
             cot_turn(level + 1)
         hand_on(level - 1)

time: 176 us -> 187 us (1.062)
  Pallas kernels: 162 us -> 173 us
    pallas_call x1, Pallas kernels: 162 us -> 173 us  [exchange(): pl.pallas_call(functools.partial(exchange_kernel, n, scale), out_shape=(j...]
where the time goes in v5:
time: 187 us
  Pallas kernels  173 us (93%)
  other arithmetic  10.2 us (5%)
  local copies, waits for them, and re-layouts  3.07 us (2%)
    pallas_call x1, Pallas kernels, exchange(): pl.pallas_call(functools.partial(exchange_kernel, n, scale), out_shape=(j...  173 us
    broadcast_in_dim x1, other arithmetic, per_device(): inner_weights[None]  10.2 us

profile of v5, /device:TPU:0, one launch (start us, length us, event | category | flops | bytes accessed | tf_op | source)
XLA Modules:
  0.0 186.7 jit_solution(13650443129713939240)
XLA Ops:
  0.6 0.0 copy-start
  0.6 1.0 copy-done
  1.7 0.0 copy-start.1
  1.7 0.0 copy-start.2
  1.7 0.0 copy-start.4
  1.7 172.7 %shard_map.118 = (f32[1024,1024]{1,0:T(8,128)}, bf16[1024,1024]{1,0:T(8,128)(2,1)S(1)}, bf16[256,8192]{1,0:T(8,128)(2,1)}) custom-call(bf16[1,1024,1024]{2,1,0:T(8,128)(2,1)} %pg.1, bf16[1024,1024]{1,0:T(8,128)(2,1)} %anchor.1, f32[1024,1024]{1,0:T(8,128)} %moment.1, bf16[256,8192]{1,0:T(8,128)(2,1)} %inputs.1, bf16[256,1024]{1,0:T(8,128)(2,1)S(1)} %copy-done), custom_call_target="tpu_custom_call" | custom-call | flops 8589934592 | bytes 16777216 | tf_op jit(solution)/shard_map/pallas_call | solution.py:329
  174.4 0.0 copy-done.1
  174.4 0.0 copy-done.2
  174.4 0.0 copy-done.4
  174.4 0.0 copy-start.3
  174.5 10.2 %fusion.3 = (bf16[1,1024,1024]{2,1,0:T(8,128)(2,1)}, bf16[1024,1024]{1,0:T(8,128)(2,1)}, f32[1024,1024]{1,0:T(8,128)}, f32[1,1024,1024]{2,1,0:T(8,128)}, f32[1,1024,1024]{2,1,0:T(8,128)}) fusion(f32[1024,1024]{1,0:T(8,128)} %get-tuple-element.10, f32[1,1024,1024]{2,1,0:T(8,128)S(1)} %copy-done.2, f32[1,1024,1024]{2,1,0:T(8,128)} %param.11, ...), kind=kLoop, calls=%fused_computation.8 | loop fusion | flops 27262976 | bytes 37748736 | tf_op jit(solution)/shard_map/broadcast_in_dim | solution.py:394
  184.7 0.0 copy-done.3
  184.7 2.0 %copy.14 = bf16[256,8192]{1,0:T(8,128)(2,1)} copy(bf16[256,8192]{1,0:T(8,128)(2,1)S(1)} %copy-done.3) | data formatting | bytes 8388608
Async XLA Ops:
  0.6 1.0 copy-start
  1.7 172.7 %copy-start.1 = (f32[1024,1024]{1,0:T(8,128)S(1)}, f32[1024,1024]{1,0:T(8,128)}, u32[]{:S(2)}) copy-start(f32[1024,1024]{1,0:T(8,128)} %moment.1) | copy-start | bytes 12582916
  1.7 172.7 %copy-start.2 = (f32[1,1024,1024]{2,1,0:T(8,128)S(1)}, f32[1,1024,1024]{2,1,0:T(8,128)}, u32[]{:S(2)}) copy-start(f32[1,1024,1024]{2,1,0:T(8,128)} %param.10) | copy-start | bytes 12582916
  1.7 172.8 %copy-start.4 = (bf16[1024,1024]{1,0:T(8,128)(2,1)S(1)}, bf16[1024,1024]{1,0:T(8,128)(2,1)}, u32[]{:S(2)}) copy-start(bf16[1024,1024]{1,0:T(8,128)(2,1)} %anchor.1) | copy-start | bytes 6291460
  174.4 10.2 %copy-start.3 = (bf16[256,8192]{1,0:T(8,128)(2,1)S(1)}, bf16[256,8192]{1,0:T(8,128)(2,1)}, u32[]{:S(2)}) copy-start(bf16[256,8192]{1,0:T(8,128)(2,1)} %get-tuple-element.28) | copy-start | bytes 12582916
